TPU v7x, 32 devices: a whole 2x2x4 slice. The times are simulated.
32 devices in a mesh: groups: 2 (over x), row: 16 (over z, y, core).
Axes of the slice: x: 2, y: 2, z: 4, core: 2. Of those that a mesh axis runs over, the one named last changes fastest.
Arguments:
- embeddings: bfloat16 [16384, 4096], P(('groups', 'row')), parts along dimension 0, may hold values from -64 to 64
- basis: bfloat16 [4096, 256], replicated, may hold values from -0.09375 to 0.09375
- cluster_ids: int32 [16384], P(('groups', 'row')), parts along dimension 0, may hold values from 0 to 127, as said below
- member_order: int32 [16384], P(('groups', 'row')), parts along dimension 0, may hold values from 0 to 1935, as said below
- owner_map: int32 [256], P('groups'), parts along dimension 0, may hold values from 0 to 15, as said below
- counts: int32 [256], P(('groups', 'row')), parts along dimension 0, may hold values from 1 to 1936, as said below
Outputs:
- best: float32 [16384], P(('groups', 'row')), parts along dimension 0
- cluster_scores: float32 [256], P(('groups', 'row')), parts along dimension 0
There are 2 independent parts, one for each index of `groups`. A program takes and returns all parts, laid end to end along the dimension named above; an argument that names none is the same for every part. Nothing has to cross between parts.
Inputs may be any that keep to these rules, and one draw needn't show every extreme that they name: `cluster_ids`: among the documents of one device's rows, at most 128 lie in clusters of one owner; in every draw some owner gets exactly 128 from every device. `member_order`: the members of each cluster carry the numbers 0 to its count - 1, each once. `owner_map`: each owner holds exactly 8 clusters. `counts`: the number of documents with this cluster id.
All inputs are finite; a program needn't handle non-finite values.
Results may differ from a plain program's by a relative error of at most 0.00061.
Values may be sent and summed in bfloat16 or wider, within the bound.
A program may use at most 64 MiB of HBM per device.

v0:
```python
import jax
import jax.numpy as jnp
from jax import lax
from jax.sharding import PartitionSpec as P

epsilon = 1e-06


def normalize(rows, basis):
    projected = jnp.dot(rows, basis, preferred_element_type=jnp.float32)
    scale = lax.rsqrt(jnp.sum(projected * projected, axis=1, keepdims=True) + epsilon)
    return (projected * scale).astype(jnp.bfloat16)


def pair_scores(queries, keys):
    return lax.dot_general(
        queries, keys, (((1,), (1,)), ((), ())), preferred_element_type=jnp.float32
    )


def select_rows(selector, source):
    picked = lax.dot_general(
        selector, source, (((0,), (0,)), ((), ())), preferred_element_type=jnp.float32
    )
    return picked.astype(source.dtype)


def pair_maxima(vectors, groups, orders):
    row_total = vectors.shape[0]
    block_rows = min(512, row_total)

    def one_block(start):
        queries = lax.dynamic_slice_in_dim(vectors, start, block_rows)
        query_groups = lax.dynamic_slice_in_dim(groups, start, block_rows)
        query_orders = lax.dynamic_slice_in_dim(orders, start, block_rows)
        scores = pair_scores(queries, vectors)
        allowed = (groups[None, :] == query_groups[:, None]) & (
            orders[None, :] < query_orders[:, None]
        )
        return jnp.max(jnp.where(allowed, scores, jnp.float32(-1.0)), axis=1)

    starts = jnp.arange(row_total // block_rows, dtype=jnp.int32) * block_rows
    return lax.map(one_block, starts).reshape(-1)


def body(embeddings, basis, cluster_ids, member_order, owner_map, counts):
    row_count = lax.axis_size("row")
    doc_rows = cluster_ids.shape[0]
    cluster_total = owner_map.shape[0]
    capacity = 4 * doc_rows // row_count
    slot_total = row_count * capacity
    cluster_hit = cluster_ids[:, None] == lax.iota(jnp.int32, cluster_total)[None, :]
    owner_of = jnp.sum(jnp.where(cluster_hit, owner_map[None, :], 0), axis=1)
    owner_hit = owner_of[:, None] == lax.iota(jnp.int32, row_count)[None, :]
    running = jnp.cumsum(owner_hit.astype(jnp.int32), axis=0)
    rank_in = jnp.sum(jnp.where(owner_hit, running, 0), axis=1) - 1
    slot_of_doc = owner_of * capacity + rank_in
    slot_hit = slot_of_doc[:, None] == lax.iota(jnp.int32, slot_total)[None, :]
    selector = slot_hit.astype(jnp.bfloat16)
    filled = jnp.any(slot_hit, axis=0)
    send_cluster = jnp.where(
        filled, jnp.sum(jnp.where(slot_hit, cluster_ids[:, None], 0), axis=0), -1
    )
    send_order = jnp.sum(jnp.where(slot_hit, member_order[:, None], 0), axis=0)
    send_cluster = send_cluster.reshape(row_count, capacity)
    send_order = send_order.reshape(row_count, capacity)
    normalized = normalize(embeddings, basis)
    packed = select_rows(selector, normalized)
    packed = packed.reshape(row_count, capacity, normalized.shape[1])
    got_rows, got_cluster, got_order = (
        lax.all_to_all(packed, "row", split_axis=0, concat_axis=0, tiled=True),
        lax.all_to_all(send_cluster, "row", split_axis=0, concat_axis=0, tiled=True),
        lax.all_to_all(send_order, "row", split_axis=0, concat_axis=0, tiled=True),
    )
    arrived = got_rows.reshape(slot_total, -1)
    arrived_cluster = got_cluster.reshape(slot_total)
    arrived_order = got_order.reshape(slot_total)
    slot_best = pair_maxima(arrived, arrived_cluster, arrived_order)
    returned = lax.all_to_all(
        slot_best.reshape(row_count, capacity), "row", split_axis=0, concat_axis=0, tiled=True
    )
    best = jnp.sum(
        jnp.where(slot_hit, returned.reshape(slot_total)[None, :], jnp.float32(0.0)), axis=1
    )
    all_counts = lax.all_gather(counts, "row", axis=0, tiled=True)
    contrib = jnp.where(arrived_order >= 1, slot_best, jnp.float32(0.0))
    arrival_hit = arrived_cluster[:, None] == lax.iota(jnp.int32, cluster_total)[None, :]
    cluster_sum = jnp.sum(jnp.where(arrival_hit, contrib[:, None], jnp.float32(0.0)), axis=0)
    cluster_mean = cluster_sum / all_counts.astype(jnp.float32)
    owned_here = owner_map == lax.axis_index("row")
    position = jnp.cumsum(owned_here.astype(jnp.int32)) - 1
    per_owner = cluster_total // row_count
    pick_table = owned_here[None, :] & (
        position[None, :] == lax.iota(jnp.int32, per_owner)[:, None]
    )
    cluster_scores = jnp.sum(jnp.where(pick_table, cluster_mean[None, :], jnp.float32(0.0)), axis=1)
    return (best, cluster_scores)


def solution(mesh):
    in_specs = (
        P(("groups", "row"), None),
        P(),
        P(("groups", "row")),
        P(("groups", "row")),
        P("groups"),
        P(("groups", "row")),
    )
    out_specs = (P(("groups", "row")), P(("groups", "row")))
    return jax.shard_map(body, mesh=mesh, in_specs=in_specs, out_specs=out_specs, check_vma=False)
```

profile of v0, /device:TPU:0, one launch (start us, length us, event | category | flops | bytes accessed | tf_op | source)
XLA Modules:
  0.0 88.8 jit_solution(2942798242441212586)
XLA Ops:
  0.6 0.0 copy-start
  0.6 1.1 %select_reduce_fusion.5 = s32[512]{0:T(512)S(1)} fusion(s32[128]{0:T(128)} %param.12, s32[512]{0:T(512)} %param.10), kind=kLoop, calls=%fused_computation.16 | loop fusion | flops 196096 | bytes 4608 | tf_op jit(solution)/shard_map/reduce_sum | solution.py:53
  1.7 1.2 %reduce-window.18 = s32[16,4,128]{2,0,1:T(8,128)S(1)} reduce-window(s32[16,4,128]{2,0,1:T(8,128)S(1)} %fusion.9, s32[]{:T(128)} %constant.9.clone.1), window={size=1x1x128 pad=0_0x0_0x127_0}, to_apply=%region_1.2 | reduce-window | flops 1040384 | bytes 65540 | tf_op jit(solution)/shard_map/reduce-window
  2.9 0.2 slice_reduce_fusion
  3.1 0.1 fusion.8
  3.3 0.7 fusion.3
  4.0 2.4 %select_reduce_fusion.2 = (s32[2048]{0:T(1024)}, s32[2048]{0:T(1024)S(1)}) fusion(s32[512]{0:T(512)} %param.11, s32[512]{0:T(512)S(1)} %add_add_fusion, s32[512]{0:T(512)} %param.10), kind=kLoop, calls=%fused_computation.4 | loop fusion | flops 5238784 | bytes 22528 | tf_op jit(solution)/shard_map/reduce_sum | solution.py:64
  6.4 0.6 broadcast_select_fusion
  7.0 7.4 %all-to-all-start = ((s32[16,1,128]{2,1,0:T(1,128)}), s32[16,1,128]{2,1,0:T(1,128)S(1)}, u32[]{:S(2)}, u32[]{:S(2)}) async-start(s32[16,1,128]{2,1,0:T(1,128)} %bitcast.6), calls=%async_computation | async-start | bytes 16384 | tf_op jit(solution)/shard_map/all_to_all | solution.py:72
  14.4 3.5 %multiply_reduce_fusion = (f32[512]{0:T(512)S(1)}, f32[512,256]{0,1:T(8,128)S(1)}) fusion(bf16[512,4096]{1,0:T(8,128)(2,1)} %param.8, bf16[4096,256]{1,0:T(8,128)(2,1)S(1)} %copy-done), kind=kOutput, calls=%fused_computation.14 | convolution fusion | flops 1074003456 | bytes 6817792 | tf_op jit(solution)/shard_map/dot_general | solution.py:10
  17.9 0.0 copy-start.1
  17.9 0.0 copy-start.3
  17.9 0.0 copy-start.2
  17.9 2.8 %all-to-all-done = s32[16,1,128]{2,1,0:T(1,128)S(1)} async-done(((s32[16,1,128]{2,1,0:T(1,128)}), s32[16,1,128]{2,1,0:T(1,128)S(1)}, u32[]{:S(2)}, u32[]{:S(2)}) %all-to-all-start) | async-done | bytes 8224 | tf_op jit(solution)/shard_map/all_to_all | solution.py:72
  20.8 3.5 %all-to-all-start.1 = ((s32[16,1,128]{2,1,0:T(1,128)}), s32[16,1,128]{2,1,0:T(1,128)S(1)}, u32[]{:S(2)}, u32[]{:S(2)}) async-start(s32[16,1,128]{2,1,0:T(1,128)} %bitcast.9), calls=%async_computation.1 | async-start | bytes 16384 | tf_op jit(solution)/shard_map/all_to_all | solution.py:73
  24.3 1.9 %convolution_convert_fusion = bf16[2048,256]{1,0:T(8,128)(2,1)} fusion(s32[512]{0:T(512)S(1)} %add_add_fusion, f32[512,256]{0,1:T(8,128)S(1)} %get-tuple-element.66, f32[512]{0:T(512)S(1)} %add_rsqrt_fusion), kind=kOutput, calls=%fused_computation.9 | convolution fusion | flops 539754496 | bytes 1576960 | tf_op jit(solution)/shard_map/dot_general | solution.py:22
  26.2 4.5 %all-to-all-done.1 = s32[16,1,128]{2,1,0:T(1,128)S(1)} async-done(((s32[16,1,128]{2,1,0:T(1,128)}), s32[16,1,128]{2,1,0:T(1,128)S(1)}, u32[]{:S(2)}, u32[]{:S(2)}) %all-to-all-start.1) | async-done | bytes 8224 | tf_op jit(solution)/shard_map/all_to_all | solution.py:73
  30.7 3.7 %all-to-all-start.2 = ((bf16[16,128,256]{2,1,0:T(8,128)(2,1)}), bf16[16,128,256]{2,1,0:T(8,128)(2,1)S(1)}, u32[]{:S(2)}, u32[]{:S(2)}) async-start(bf16[16,128,256]{2,1,0:T(8,128)(2,1)} %bitcast.48), calls=%async_computation.2 | async-start | bytes 2097152 | tf_op jit(solution)/shard_map/all_to_all | solution.py:71
  34.4 0.1 copy.14
  34.5 0.2 reduce-window.20
  34.6 0.6 dynamic-slice
  35.9 0.2 dynamic-update-slice
  36.1 24.8 %all-reduce = s32[128]{0:T(128)S(1)} all-reduce(s32[128]{0:T(128)S(1)} %dynamic-update-slice), channel_id=1, replica_groups=mesh['groups'=2,'row'=16] {'row'}, use_global_device_ids=true, to_apply=%add | all-reduce | flops 128 | bytes 1024
  61.0 0.1 add_reduce_fusion
  61.1 0.0 all-to-all-done.2
  61.1 15.0 %while.10 = (s32[]{:T(128)}, f32[4,512]{1,0:T(4,128)S(1)}, s32[16,128]{1,0:T(8,128)S(1)}, s32[4]{0:T(128)S(1)}, s32[2048]{0:T(1024)S(1)}, /*index=5*/s32[16,128]...) while((s32[]{:T(128)}, f32[4,512]{1,0:T(4,128)S(1)}, ...), condition=%wide.region_10.11_spmd, body=%wide.region_8.10_spmd.sunk | while | flops 542113280 | bytes 1345707 | solution.py:43
  61.1 0.6 dynamic_slice.20
  63.6 0.1 dynamic_slice.21
  63.7 0.1 dynamic_slice.22
  63.8 1.0 %select_reduce_fusion.8 = f32[512]{0:T(512)S(1)} fusion(bf16[2048,256]{1,0:T(8,128)(2,1)S(1)} %get-tuple-element.145, s32[2048]{0:T(1024)S(1)} %get-tuple-element.144, s32[2048]{0:T(1024)S(1)} %get-tuple-element.142, s32[512]{0:T(512)S(1)} %dynamic_slice.21, s32[512]{0:T(512)S(1)} %dynamic_slice.22, s32[]{:T(128)S(6)} %select_n.84), kind=kOutput, calls=%fused_computation.clone.1 | convolution fusion | flops 542113280 | bytes 1333252 | tf_op jit(solution)/shard_map/while/body/eval_jaxpr/dot_general | solution.py:16
  64.8 0.6 dynamic_slice.20
  67.4 0.1 dynamic_slice.21
  67.5 0.1 dynamic_slice.22
  67.5 1.0 %select_reduce_fusion.8 = f32[512]{0:T(512)S(1)} fusion(bf16[2048,256]{1,0:T(8,128)(2,1)S(1)} %get-tuple-element.145, s32[2048]{0:T(1024)S(1)} %get-tuple-element.144, s32[2048]{0:T(1024)S(1)} %get-tuple-element.142, s32[512]{0:T(512)S(1)} %dynamic_slice.21, s32[512]{0:T(512)S(1)} %dynamic_slice.22, s32[]{:T(128)S(6)} %select_n.84), kind=kOutput, calls=%fused_computation.clone.1 | convolution fusion | flops 542113280 | bytes 1333252 | tf_op jit(solution)/shard_map/while/body/eval_jaxpr/dot_general | solution.py:16
  68.6 0.6 dynamic_slice.20
  71.1 0.1 dynamic_slice.21
  71.2 0.1 dynamic_slice.22
  71.3 1.0 %select_reduce_fusion.8 = f32[512]{0:T(512)S(1)} fusion(bf16[2048,256]{1,0:T(8,128)(2,1)S(1)} %get-tuple-element.145, s32[2048]{0:T(1024)S(1)} %get-tuple-element.144, s32[2048]{0:T(1024)S(1)} %get-tuple-element.142, s32[512]{0:T(512)S(1)} %dynamic_slice.21, s32[512]{0:T(512)S(1)} %dynamic_slice.22, s32[]{:T(128)S(6)} %select_n.84), kind=kOutput, calls=%fused_computation.clone.1 | convolution fusion | flops 542113280 | bytes 1333252 | tf_op jit(solution)/shard_map/while/body/eval_jaxpr/dot_general | solution.py:16
  72.3 0.6 dynamic_slice.20
  74.9 0.1 dynamic_slice.21
  74.9 0.1 dynamic_slice.22
  75.0 1.0 %select_reduce_fusion.8 = f32[512]{0:T(512)S(1)} fusion(bf16[2048,256]{1,0:T(8,128)(2,1)S(1)} %get-tuple-element.145, s32[2048]{0:T(1024)S(1)} %get-tuple-element.144, s32[2048]{0:T(1024)S(1)} %get-tuple-element.142, s32[512]{0:T(512)S(1)} %dynamic_slice.21, s32[512]{0:T(512)S(1)} %dynamic_slice.22, s32[]{:T(128)S(6)} %select_n.84), kind=kOutput, calls=%fused_computation.clone.1 | convolution fusion | flops 542113280 | bytes 1333252 | tf_op jit(solution)/shard_map/while/body/eval_jaxpr/dot_general | solution.py:16
  76.1 0.6 all_to_all.29
  76.7 0.7 select_reduce_fusion.4
  77.4 3.7 %all-to-all-start.3 = ((f32[16,1,128]{2,1,0:T(1,128)}), f32[16,1,128]{2,1,0:T(1,128)S(1)}, u32[]{:S(2)}, u32[]{:S(2)}) async-start(f32[16,1,128]{2,1,0:T(1,128)} %all_to_all.29), calls=%async_computation.3 | async-start | bytes 16384 | tf_op jit(solution)/shard_map/all_to_all | solution.py:79
  81.1 0.6 select_reduce_fusion.6
  81.7 5.8 %all-to-all-done.3 = f32[16,1,128]{2,1,0:T(1,128)S(1)} async-done(((f32[16,1,128]{2,1,0:T(1,128)}), f32[16,1,128]{2,1,0:T(1,128)S(1)}, u32[]{:S(2)}, u32[]{:S(2)}) %all-to-all-start.3) | async-done | bytes 8224 | tf_op jit(solution)/shard_map/all_to_all | solution.py:79
  87.5 1.2 %select_reduce_fusion.1 = f32[512]{0:T(512)} fusion(f32[2048]{0:T(1024)S(1)} %bitcast.59, s32[512]{0:T(512)S(1)} %add_add_fusion), kind=kLoop, calls=%fused_computation.3 | loop fusion | flops 3145216 | bytes 12288 | tf_op jit(solution)/shard_map/reduce_sum | solution.py:82
  (20 shorter events, 0.3 us)
Async XLA Ops:
  0.6 13.8 %copy-start = (bf16[4096,256]{1,0:T(8,128)(2,1)S(1)}, bf16[4096,256]{1,0:T(8,128)(2,1)}, u32[]{:S(2)}) copy-start(bf16[4096,256]{1,0:T(8,128)(2,1)} %param.9) | copy-start | bytes 6291460
  7.0 13.8 %all-to-all-start = ((s32[16,1,128]{2,1,0:T(1,128)}), s32[16,1,128]{2,1,0:T(1,128)S(1)}, u32[]{:S(2)}, u32[]{:S(2)}) async-start(s32[16,1,128]{2,1,0:T(1,128)} %bitcast.6), calls=%async_computation | async-start | bytes 16384 | tf_op jit(solution)/shard_map/all_to_all | solution.py:72
  17.9 16.4 %copy-start.1 = (s32[128]{0:T(128)S(1)}, s32[128]{0:T(128)}, u32[]{:S(2)}) copy-start(s32[128]{0:T(128)} %param.12) | copy-start | bytes 1540
  17.9 16.7 %copy-start.3 = (u32[32]{0:T(128)S(1)}, u32[32]{0:T(128)}, u32[]{:S(2)}) copy-start(u32[32]{0:T(128)} %constant.48) | copy-start | bytes 388
  17.9 18.0 %copy-start.2 = (s32[8]{0:T(128)S(1)}, s32[8]{0:T(128)}, u32[]{:S(2)}) copy-start(s32[8]{0:T(128)} %param.13) | copy-start | bytes 100
  20.8 9.9 %all-to-all-start.1 = ((s32[16,1,128]{2,1,0:T(1,128)}), s32[16,1,128]{2,1,0:T(1,128)S(1)}, u32[]{:S(2)}, u32[]{:S(2)}) async-start(s32[16,1,128]{2,1,0:T(1,128)} %bitcast.9), calls=%async_computation.1 | async-start | bytes 16384 | tf_op jit(solution)/shard_map/all_to_all | solution.py:73
  30.7 30.4 %all-to-all-start.2 = ((bf16[16,128,256]{2,1,0:T(8,128)(2,1)}), bf16[16,128,256]{2,1,0:T(8,128)(2,1)S(1)}, u32[]{:S(2)}, u32[]{:S(2)}) async-start(bf16[16,128,256]{2,1,0:T(8,128)(2,1)} %bitcast.48), calls=%async_computation.2 | async-start | bytes 2097152 | tf_op jit(solution)/shard_map/all_to_all | solution.py:71
  77.4 10.1 %all-to-all-start.3 = ((f32[16,1,128]{2,1,0:T(1,128)}), f32[16,1,128]{2,1,0:T(1,128)S(1)}, u32[]{:S(2)}, u32[]{:S(2)}) async-start(f32[16,1,128]{2,1,0:T(1,128)} %all_to_all.29), calls=%async_computation.3 | async-start | bytes 16384 | tf_op jit(solution)/shard_map/all_to_all | solution.py:79
where the time goes:
time: 89.3 us; the launch traced here: 88.8 us
  blocking collectives  24.8 us (28%)
  starting transfers between devices  18.2 us (20%)
  waiting for transfers between devices  13.1 us (15%)
  matrix products  9.35 us (10%)
  other arithmetic  8.98 us (10%)
  loops' own time  7.85 us (9%)
  local copies, waits for them, and re-layouts  4.96 us (6%)
  between operations  1.47 us (2%)
    unnamed x1, blocking collectives  24.8 us
    another operation x1, loops' own time, pair_maxima(): return lax.map(one_block, starts).reshape(-1)  7.85 us
    all_to_all x1, starting transfers between devices, body(): lax.all_to_all(send_cluster, 'row', split_axis=0, concat_axis=0, tiled=True)  7.39 us
    all_to_all x1, waiting for transfers between devices, body(): lax.all_to_all(slot_best.reshape(row_count, capacity), 'row', split_axis=...  5.77 us
    all_to_all x1, waiting for transfers between devices, body(): lax.all_to_all(send_order, 'row', split_axis=0, concat_axis=0, tiled=True)  4.47 us
    dot_general x4, matrix products, pair_scores(): lax.dot_general(queries, keys, (((1,), (1,)), ((), ())), preferred_elemen...  3.95 us
    all_to_all x1, starting transfers between devices, body(): lax.all_to_all(slot_best.reshape(row_count, capacity), 'row', split_axis=...  3.72 us
    all_to_all x1, starting transfers between devices, body(): lax.all_to_all(packed, 'row', split_axis=0, concat_axis=0, tiled=True)  3.65 us
  transfers between devices with their start and end apart: 4, of which 3 were waited for; matrix products, arithmetic and copies ran while one was open for 8% of the time, Pallas kernels for 0%

commit v1 on v0

v1 whole, which is shorter than its diff:
```python
import functools

import jax
import jax.numpy as jnp
from jax import lax
from jax.experimental import pallas as pl
from jax.experimental.pallas import tpu as pltpu
from jax.sharding import PartitionSpec as P

epsilon = 1e-06
MESH = pl.DeviceIdType.MESH
CHUNKS = 2


def row_of(tile, reduce):
    pieces = [
        reduce(jnp.transpose(tile[i : i + 128, :]), axis=0, keepdims=True)
        for i in range(0, tile.shape[0], 128)
    ]
    return pieces[0] if len(pieces) == 1 else jnp.concatenate(pieces, axis=1)


def kernel(
    n, lines, emb_hbm, basis_hbm, meta_ref, owner_ref,
    best_ref, scores_ref,
    emb, basis, blk, meta, kcol, ccol, acc, col, row, home, rr, rc, part,
    load_sem, basis_sem, own_send, plane_recv, fwd_plane, line_recv, fwd_send,
    meta_send, meta_recv, row_send, row_recv, col_send, col_recv, part_send, part_recv,
):
    planes = n // lines
    half = planes // 2
    docs = blk.shape[1]
    size = docs // CHUNKS
    clusters = owner_ref.shape[1]
    order_bits = (n * docs - 1).bit_length()
    group_of = lambda keys: lax.shift_right_logical(keys, order_bits)
    me = lax.axis_index("row")
    z = me // lines
    line = me % lines

    def from_below(s, at):
        return (s >= 0) & (s < half) & (s < at) & (at <= planes - 2)

    def from_above(s, at):
        return (s < planes) & (at < s) & (at >= 0) & ((s == planes - 1) | ((s >= half) & (at >= half)))

    def piece(d, c):
        return blk.at[d, pl.ds(c * size, size)]

    def remote(src, dst, send, recv, device):
        return pltpu.make_async_remote_copy(
            src_ref=src, dst_ref=dst, send_sem=send, recv_sem=recv,
            device_id={"row": device}, device_id_type=MESH,
        )

    def block_copy(d, c, send, recv, device):
        return remote(piece(d, c), piece(d, c), send, recv, device)

    basis_copy = pltpu.make_async_copy(basis_hbm, basis, basis_sem)
    basis_copy.start()
    loads = []
    for c in range(CHUNKS):
        part_rows = pl.ds(c * size, size)
        load = pltpu.make_async_copy(emb_hbm.at[part_rows], emb.at[part_rows], load_sem.at[c])
        load.start()
        loads.append(load)

    barrier = pltpu.get_barrier_semaphore()

    @pl.loop(1, n)
    def _(k):
        pl.semaphore_signal(barrier, inc=1, device_id={"row": (me + k) % n}, device_id_type=MESH)

    pl.semaphore_wait(barrier, n - 1)

    meta[me] = meta_ref[...]

    def meta_copy(k):
        return remote(meta.at[me], meta.at[me], meta_send.at[k], meta_recv.at[me], (me + k) % n)

    @pl.loop(1, n)
    def _(k):
        meta_copy(k).start()

    goes_up = from_below(z, z + 1)
    goes_down = from_above(z, z - 1)

    def own_copies(c):
        copies = [(None, block_copy(me, c, own_send.at[0, c], plane_recv.at[line, c], me ^ 1))]
        if lines == 4:
            copies.append((None, block_copy(me, c, own_send.at[1, c], plane_recv.at[line, c], me ^ 2)))
        if planes > 1:
            up = jnp.minimum(me + lines, n - 1)
            down = jnp.maximum(me - lines, 0)
            copies.append((goes_up, block_copy(me, c, own_send.at[2, c], line_recv.at[z, c], up)))
            copies.append((goes_down, block_copy(me, c, own_send.at[3, c], line_recv.at[z, c], down)))
        return copies

    def each(copies, act):
        for condition, copy in copies:
            if condition is None:
                act(copy)
            else:
                pl.when(condition)(functools.partial(act, copy))

    basis_copy.wait()
    for c in range(CHUNKS):
        loads[c].wait()
        projected = jnp.dot(
            emb[pl.ds(c * size, size), :], basis[...], preferred_element_type=jnp.float32
        )
        scale = lax.rsqrt(jnp.sum(projected * projected, axis=1, keepdims=True) + epsilon)
        blk[me, pl.ds(c * size, size), :] = (projected * scale).astype(jnp.bfloat16)
        each(own_copies(c)[::-1], lambda copy: copy.start())

    @pl.loop(1, n)
    def _(k):
        d = (me + k) % n
        remote(meta.at[d], meta.at[d], meta_send.at[k], meta_recv.at[d], d).wait_recv()

    for p in range(lines):
        keys = meta[z * lines + p][:, :docs]
        for i in range(0, docs, 128):
            column = jnp.transpose(jnp.broadcast_to(keys[:, i : i + 128], (128, 128)))
            kcol[pl.ds(p * docs + i, 128), :] = column
            ccol[pl.ds(p * docs + i, 128), :] = group_of(column)
    acc[...] = jnp.full_like(acc, -1.0)

    def plane_wait(p, c):
        block_copy(z * lines + p, c, own_send.at[0, c], plane_recv.at[p, c], me ^ 1).wait_recv()

    def line_wait(s, c):
        block_copy(s * lines + line, c, own_send.at[0, c], line_recv.at[s, c], me ^ 1).wait_recv()

    def forward(s, c, device):
        return block_copy(s * lines + line, c, fwd_send.at[s, c], line_recv.at[s, c], device)

    def arrivals(k):
        low, high = z - k, z + k
        below = from_below(low, z)
        above = from_above(high, z)
        return (
            (jnp.maximum(low, 0), below, below & from_below(low, z + 1), jnp.minimum(me + lines, n - 1)),
            (jnp.minimum(high, planes - 1), above, above & from_above(high, z - 1), jnp.maximum(me - lines, 0)),
        )

    def forward_step(k, c):
        for s, _, on, device in arrivals(k):
            @pl.when(on)
            def _():
                line_wait(s, c)
                forward(s, c, device).start()

    def diagonal_copy(c):
        return block_copy(me ^ 2, c, fwd_plane.at[c], plane_recv.at[line ^ 2, c], me ^ 1)

    for c in range(CHUNKS):
        forward_step(1, c)
        if lines == 4:
            plane_wait(line ^ 2, c)
            diagonal_copy(c).start()
    for c in range(CHUNKS):
        plane_wait(line ^ 1, c)
        if lines == 4:
            plane_wait(line ^ 3, c)

    def process(d, s, c, visitor):
        keys = blk[d, pl.ds(c * size, size), :]
        at = pl.ds(pl.multiple_of(c * size, size), size)
        lane_keys = meta[d, :, at]
        lane_groups = group_of(lane_keys)

        def one(p, carry):
            scores = lax.dot_general(
                blk[z * lines + p], keys, (((1,), (1,)), ((), ())), preferred_element_type=jnp.float32
            )
            rows = pl.ds(pl.multiple_of(p * docs, docs), docs)
            k_col, c_col = kcol[rows, :], ccol[rows, :]
            row_part = acc[rows, :] if visitor else None
            outs = []
            for i in range(0, size, 128):
                lk, lg = lane_keys[:, i : i + 128], lane_groups[:, i : i + 128]
                s_same = jnp.where(c_col == lg, scores[:, i : i + 128], -1.0)
                if visitor:
                    earlier = lk < k_col
                    row_part = jnp.maximum(row_part, jnp.where(earlier, s_same, -1.0))
                    for_lane = jnp.where(earlier, -1.0, s_same)
                else:
                    for_lane = jnp.where(k_col < lk, s_same, -1.0)
                outs.append(jnp.max(for_lane, axis=0, keepdims=True))
            if visitor:
                acc[rows, :] = row_part
            return jnp.maximum(carry, jnp.concatenate(outs, axis=1))

        result = lax.fori_loop(0, lines, one, jnp.full((1, size), -1.0, jnp.float32))
        if visitor:
            col[s, :, at] = result
        else:
            home[:, at] = result

    def col_copy(s, at, device):
        return remote(col.at[s], rc.at[at], col_send.at[s], col_recv.at[at], device)

    def process_step(k):
        for s, here, on, _ in arrivals(k):
            @pl.when(here)
            def _():
                @pl.loop(0, CHUNKS)
                def _(c):
                    @pl.when(jnp.logical_not(on))
                    def _():
                        line_wait(s, c)
                    process(s * lines + line, s, c, True)
                col_copy(s, z, s * lines + line).start()

    if planes > 2:
        forward_step(2, 0)

    @pl.loop(0, CHUNKS)
    def _(c):
        process(me, z, c, False)

    if planes > 2:
        for c in range(1, CHUNKS):
            forward_step(2, c)
    if planes > 1:
        process_step(1)

        @pl.loop(2, planes)
        def _(k):
            for c in range(CHUNKS):
                forward_step(k + 1, c)
            process_step(k)

    for p in range(lines):
        row[p] = row_of(acc[p * docs : (p + 1) * docs, :], jnp.max)

    def row_copy(q):
        return remote(row.at[line ^ q], rr.at[line], row_send.at[q], row_recv.at[line], me ^ q)

    for q in range(1, lines):
        row_copy(q).start()
    home[...] = jnp.maximum(home[...], row[line])
    for q in range(1, lines):
        remote(row.at[line], rr.at[line ^ q], row_send.at[q], row_recv.at[line ^ q], me ^ q).wait_recv()
        home[...] = jnp.maximum(home[...], rr[line ^ q])

    @pl.loop(0, planes)
    def _(at):
        @pl.when(from_below(z, at) | from_above(z, at))
        def _():
            remote(col.at[z], rc.at[at], col_send.at[z], col_recv.at[at], me ^ 1).wait_recv()
            home[...] = jnp.maximum(home[...], rc[at])

    best = home[...]
    best_ref[...] = best

    own_keys = meta[me][:, :docs]
    own_groups = group_of(own_keys)
    adds = jnp.where(own_keys - lax.shift_left(own_groups, order_bits) >= 1, best, 0.0)
    for i in range(0, clusters, 128):
        ids = lax.broadcasted_iota(jnp.int32, (128, 128), 0) + i
        total = jnp.zeros((128, 128), jnp.float32)
        for j in range(0, docs, 128):
            total += jnp.where(ids == own_groups[:, j : j + 128], adds[:, j : j + 128], 0.0)
        part[me, :, i : i + 128] = row_of(total, jnp.sum)

    def part_copy(k):
        return remote(part.at[me], part.at[me], part_send.at[k], part_recv.at[me], (me + k) % n)

    @pl.loop(1, n)
    def _(k):
        part_copy(k).start()

    owned = (owner_ref[...] == me).astype(jnp.float32)
    before = (
        lax.broadcasted_iota(jnp.int32, (clusters, clusters), 0)
        < lax.broadcasted_iota(jnp.int32, (clusters, clusters), 1)
    ).astype(jnp.bfloat16)
    per_owner = clusters // n
    many = jnp.broadcast_to(owned, (per_owner, clusters))
    rank = jnp.dot(many.astype(jnp.bfloat16), before, preferred_element_type=jnp.float32)
    wanted = lax.broadcasted_iota(jnp.int32, (per_owner, clusters), 0).astype(jnp.float32)
    pick = (many > 0.5) & (rank == wanted)

    @pl.loop(1, n)
    def _(k):
        d = (me + k) % n
        remote(part.at[d], part.at[d], part_send.at[k], part_recv.at[d], d).wait_recv()

    sums = jnp.zeros((1, clusters), jnp.float32)
    counts = jnp.zeros((1, clusters), jnp.int32)
    for d in range(n):
        sums += part[d]
        counts += meta[d][:, docs:]
    mean = sums / counts.astype(jnp.float32)
    scores_ref[...] = jnp.sum(jnp.where(pick, mean, 0.0), axis=1, keepdims=True)

    for c in range(CHUNKS):
        each(own_copies(c), lambda copy: copy.wait_send())
        if lines == 4:
            diagonal_copy(c).wait_send()

    @pl.loop(1, n)
    def _(k):
        meta_copy(k).wait_send()
        part_copy(k).wait_send()

    for q in range(1, lines):
        row_copy(q).wait_send()

    @pl.loop(1, planes)
    def _(k):
        for s, here, on, device in arrivals(k):
            @pl.when(here)
            def _():
                col_copy(s, z, s * lines + line).wait_send()

            @pl.when(on)
            def _():
                for c in range(CHUNKS):
                    forward(s, c, device).wait_send()


def body(embeddings, basis, cluster_ids, member_order, owner_map, counts):
    n = lax.axis_size("row")
    docs, width = embeddings.shape
    kept = basis.shape[1]
    clusters = owner_map.shape[0]
    lines = 4 if n <= 16 else 2
    planes = n // lines
    share = counts.shape[0]
    lane = lax.iota(jnp.int32, clusters)
    placed = jnp.where(lane // share == lax.axis_index("row"), jnp.tile(counts, n), 0)
    meta = jnp.concatenate([(cluster_ids << (n * docs - 1).bit_length()) + member_order, placed]).reshape(1, -1)
    vmem = functools.partial(pl.BlockSpec, memory_space=pltpu.VMEM)
    hbm = functools.partial(pl.BlockSpec, memory_space=pl.ANY)
    dma = pltpu.SemaphoreType.DMA
    f32, i32, bf16 = jnp.float32, jnp.int32, jnp.bfloat16
    best, scores = pl.pallas_call(
        functools.partial(kernel, n, lines),
        out_shape=(
            jax.ShapeDtypeStruct((1, docs), f32),
            jax.ShapeDtypeStruct((clusters // n, 1), f32),
        ),
        in_specs=[hbm(), hbm(), vmem(), vmem()],
        out_specs=(vmem(), vmem()),
        scratch_shapes=[
            pltpu.VMEM((docs, width), bf16),
            pltpu.VMEM((width, kept), bf16),
            pltpu.VMEM((n, docs, kept), bf16),
            pltpu.VMEM((n, 1, docs + clusters), i32),
            pltpu.VMEM((lines * docs, 128), i32),
            pltpu.VMEM((lines * docs, 128), i32),
            pltpu.VMEM((lines * docs, 128), f32),
            pltpu.VMEM((planes, 1, docs), f32),
            pltpu.VMEM((lines, 1, docs), f32),
            pltpu.VMEM((1, docs), f32),
            pltpu.VMEM((lines, 1, docs), f32),
            pltpu.VMEM((planes, 1, docs), f32),
            pltpu.VMEM((n, 1, clusters), f32),
            dma((CHUNKS,)),
            dma,
            dma((4, CHUNKS)),
            dma((lines, CHUNKS)),
            dma((CHUNKS,)),
            dma((planes, CHUNKS)),
            dma((planes, CHUNKS)),
            dma((n,)),
            dma((n,)),
            dma((lines,)),
            dma((lines,)),
            dma((planes,)),
            dma((planes,)),
            dma((n,)),
            dma((n,)),
        ],
        compiler_params=pltpu.CompilerParams(
            collective_id=0, has_side_effects=True, vmem_limit_bytes=48 * 1024 * 1024
        ),
        name="cluster_scores",
    )(embeddings, basis, meta, owner_map.reshape(1, -1))
    return best.reshape(-1), scores.reshape(-1)


def solution(mesh):
    in_specs = (
        P(("groups", "row"), None),
        P(),
        P(("groups", "row")),
        P(("groups", "row")),
        P("groups"),
        P(("groups", "row")),
    )
    out_specs = (P(("groups", "row")), P(("groups", "row")))
    return jax.shard_map(body, mesh=mesh, in_specs=in_specs, out_specs=out_specs, check_vma=False)
```

time: 89.3 us -> 39.6 us (0.44)
  Pallas kernels: 0 us -> 33.9 us
  blocking collectives: 24.8 us -> 0 us
  starting transfers between devices: 18.2 us -> 0 us
  waiting for transfers between devices: 13.1 us -> 0 us
  matrix products: 9.35 us -> 0 us
  loops' own time: 7.85 us -> 0 us
  other arithmetic: 8.98 us -> 1.34 us
  local copies, waits for them, and re-layouts: 4.96 us -> 3.57 us
    pallas_call x0 -> x1, Pallas kernels: none -> 33.9 us  [body(): pl.pallas_call(functools.partial(kernel, n, lines), out_shape=(jax.ShapeD...]
    unnamed x1 -> x0, blocking collectives: 24.8 us -> none
    all_to_all x4 -> x0, starting transfers between devices: 18.2 us -> none  [the longest x1 7.39 us: body(): lax.all_to_all(send_cluster, 'row', split_axis=0, concat_axis=0, tiled=True)]
    all_to_all x4 -> x0, waiting for transfers between devices: 13.1 us -> none  [the longest x1 5.77 us: body(): lax.all_to_all(slot_best.reshape(row_count, capacity), 'row', split_axis=...]
    dot_general x6 -> x0, matrix products: 9.35 us -> none  [the longest x4 3.95 us: pair_scores(): lax.dot_general(queries, keys, (((1,), (1,)), ((), ())), preferred_elemen...]
    another operation x1 -> x0, loops' own time: 7.85 us -> none  [pair_maxima(): return lax.map(one_block, starts).reshape(-1)]
    reduce_sum x6 -> x0, other arithmetic: 6.13 us -> none  [the longest x1 2.38 us: body(): send_order = jnp.sum(jnp.where(slot_hit, member_order[:, None], 0), axis=0)]
    dynamic_slice x12 -> x0, local copies, waits for them, and re-layouts: 2.96 us -> none  [the longest x4 2.35 us: pair_maxima(): return lax.map(one_block, starts).reshape(-1)]
  transfers between devices with their start and end apart: 4 -> 0, of which waited for: 3 -> 0; matrix products, arithmetic and copies ran while one was open for 8% -> 0% of each run, Pallas kernels for 0% -> 0%
where the time goes in v1:
time: 39.6 us; the launch traced here: 39.4 us
  Pallas kernels  33.9 us (86%)
  local copies, waits for them, and re-layouts  3.57 us (9%)
  other arithmetic  1.34 us (3%)
  between operations  0.67 us (2%)
    pallas_call x1, Pallas kernels, body(): pl.pallas_call(functools.partial(kernel, n, lines), out_shape=(jax.ShapeD...  33.9 us
    unnamed x5, local copies, waits for them, and re-layouts  2.82 us

profile of v1, /device:TPU:0, one launch (start us, length us, event | category | flops | bytes accessed | tf_op | source)
XLA Modules:
  0.0 39.4 jit_solution(12426711825262218091)
XLA Ops:
  0.6 0.7 %tile.4 = s32[16,8]{1,0:T(8,128)S(1)} broadcast(s32[8]{0:T(128)} %param.11), dimensions={1} | broadcast | bytes 544 | tf_op jit(solution)/shard_map/tile | solution.py:334
  1.3 0.1 tile.10
  1.4 0.7 %shift-left_add_fusion = s32[512]{0:T(512)S(1)} fusion(s32[512]{0:T(512)} %param.9, s32[512]{0:T(512)} %param.8), kind=kLoop, calls=%fused_computation.1 | loop fusion | flops 1024 | bytes 6144 | tf_op jit(solution)/shard_map/add | solution.py:335
  2.1 0.0 copy-start
  2.1 1.6 %copy-done = bf16[4096,256]{1,0:T(8,128)(2,1)S(1)} copy-done((bf16[4096,256]{1,0:T(8,128)(2,1)S(1)}, bf16[4096,256]{1,0:T(8,128)(2,1)}, u32[]{:S(2)}) %copy-start) | copy-done | bytes 2097176
  3.7 0.0 copy-start.1
  3.7 0.7 %copy-done.1 = s32[128]{0:T(128)S(1)} copy-done((s32[128]{0:T(128)S(1)}, s32[128]{0:T(128)}, u32[]{:S(2)}) %copy-start.1) | copy-done | bytes 536
  4.4 33.9 %cluster_scores.1 = (f32[1,512]{1,0:T(1,128)S(1)}, f32[8,1]{1,0:T(8,128)S(1)}) custom-call(bf16[512,4096]{1,0:T(8,128)(2,1)} %emb_hbm.1, bf16[4096,256]{1,0:T(8,128)(2,1)S(1)} %copy-done, s32[1,640]{1,0:T(1,128)S(1)} %reshape.17.meta_ref, s32[1,128]{1,0:T(1,128)S(1)} %bitcast.3), custom_call_target="tpu_custom_call" | custom-call | tf_op jit(solution)/shard_map/cluster_scores/pallas_call | solution.py:340
  38.2 0.6 %reduce = f32[8]{0:T(128)} reduce(f32[8,1]{1,0:T(8,128)S(1)} %get-tuple-element.5, f32[]{:T(128)} %constant.26), dimensions={1}, to_apply=%get-tuple-element.5.reduce_sub_computation | reduce | bytes 68 | tf_op jit(solution)/shard_map/cluster_scores/pallas_call | solution.py:340
  38.9 0.6 %copy.9 = f32[512]{0:T(512)} copy(f32[512]{0:T(512)S(1)} %bitcast.2) | data formatting | bytes 4096
  (3 shorter events, 0.0 us)
Async XLA Ops:
  2.1 1.6 %copy-start = (bf16[4096,256]{1,0:T(8,128)(2,1)S(1)}, bf16[4096,256]{1,0:T(8,128)(2,1)}, u32[]{:S(2)}) copy-start(bf16[4096,256]{1,0:T(8,128)(2,1)} %basis_hbm.1) | copy-start | bytes 6291460
  3.7 0.7 %copy-start.1 = (s32[128]{0:T(128)S(1)}, s32[128]{0:T(128)}, u32[]{:S(2)}) copy-start(s32[128]{0:T(128)} %param.10) | copy-start | bytes 1540

commit v2 on v1

--- a/solution.py
+++ b/solution.py
@@ -21,17 +21,18 @@
 
 
 def kernel(
-    n, lines, emb_hbm, basis_hbm, meta_ref, owner_ref,
+    n, lines, emb_hbm, basis_hbm, ids_hbm, order_hbm, owner_hbm, counts_hbm,
     best_ref, scores_ref,
-    emb, basis, blk, meta, kcol, ccol, acc, col, row, home, rr, rc, part,
-    load_sem, basis_sem, own_send, plane_recv, fwd_plane, line_recv, fwd_send,
+    ids, order, owner, counts_here, emb, basis, blk, meta, kcol, ccol, acc, col, row, home, rr, rc, part,
+    small_sem, load_sem, basis_sem, own_send, plane_recv, fwd_plane, line_recv, fwd_send,
     meta_send, meta_recv, row_send, row_recv, col_send, col_recv, part_send, part_recv,
 ):
     planes = n // lines
     half = planes // 2
     docs = blk.shape[1]
     size = docs // CHUNKS
-    clusters = owner_ref.shape[1]
+    clusters = owner_hbm.shape[0]
+    share = counts_hbm.shape[0]
     order_bits = (n * docs - 1).bit_length()
     group_of = lambda keys: lax.shift_right_logical(keys, order_bits)
     me = lax.axis_index("row")
@@ -56,6 +57,14 @@
     def block_copy(d, c, send, recv, device):
         return remote(piece(d, c), piece(d, c), send, recv, device)
 
+    smalls = [
+        pltpu.make_async_copy(source, target, small_sem.at[i])
+        for i, (source, target) in enumerate(
+            ((ids_hbm, ids), (order_hbm, order), (owner_hbm, owner), (counts_hbm, counts_here))
+        )
+    ]
+    for copy in smalls:
+        copy.start()
     basis_copy = pltpu.make_async_copy(basis_hbm, basis, basis_sem)
     basis_copy.start()
     loads = []
@@ -73,7 +82,16 @@
 
     pl.semaphore_wait(barrier, n - 1)
 
-    meta[me] = meta_ref[...]
+    for copy in smalls:
+        copy.wait()
+    own_ids = ids[...].reshape(1, docs)
+    own_order = order[...].reshape(1, docs)
+    meta[me, :, :docs] = lax.shift_left(own_ids, order_bits) + own_order
+    lane = lax.broadcasted_iota(jnp.int32, (1, clusters), 1) - me * share
+    placed = jnp.zeros((1, clusters), jnp.int32)
+    for k in range(share):
+        placed = jnp.where(lane == k, counts_here[k], placed)
+    meta[me, :, docs:] = placed
 
     def meta_copy(k):
         return remote(meta.at[me], meta.at[me], meta_send.at[k], meta_recv.at[me], (me + k) % n)
@@ -255,14 +273,12 @@
     best = home[...]
     best_ref[...] = best
 
-    own_keys = meta[me][:, :docs]
-    own_groups = group_of(own_keys)
-    adds = jnp.where(own_keys - lax.shift_left(own_groups, order_bits) >= 1, best, 0.0)
+    adds = jnp.where(own_order >= 1, best, 0.0)
     for i in range(0, clusters, 128):
-        ids = lax.broadcasted_iota(jnp.int32, (128, 128), 0) + i
+        ids_row = lax.broadcasted_iota(jnp.int32, (128, 128), 0) + i
         total = jnp.zeros((128, 128), jnp.float32)
         for j in range(0, docs, 128):
-            total += jnp.where(ids == own_groups[:, j : j + 128], adds[:, j : j + 128], 0.0)
+            total += jnp.where(ids_row == own_ids[:, j : j + 128], adds[:, j : j + 128], 0.0)
         part[me, :, i : i + 128] = row_of(total, jnp.sum)
 
     def part_copy(k):
@@ -272,7 +288,7 @@
     def _(k):
         part_copy(k).start()
 
-    owned = (owner_ref[...] == me).astype(jnp.float32)
+    owned = (owner[...].reshape(1, clusters) == me).astype(jnp.float32)
     before = (
         lax.broadcasted_iota(jnp.int32, (clusters, clusters), 0)
         < lax.broadcasted_iota(jnp.int32, (clusters, clusters), 1)
@@ -294,7 +310,10 @@
         sums += part[d]
         counts += meta[d][:, docs:]
     mean = sums / counts.astype(jnp.float32)
-    scores_ref[...] = jnp.sum(jnp.where(pick, mean, 0.0), axis=1, keepdims=True)
+    picked = jnp.where(pick, mean, 0.0)
+    folded = sum(picked[:, i : i + 128] for i in range(0, clusters, 128))
+    rest = jnp.zeros((128 - per_owner, 128), jnp.float32)
+    scores_ref[...] = row_of(jnp.concatenate([folded, rest], axis=0), jnp.sum)[:, :per_owner]
 
     for c in range(CHUNKS):
         each(own_copies(c), lambda copy: copy.wait_send())
@@ -330,9 +349,6 @@
     lines = 4 if n <= 16 else 2
     planes = n // lines
     share = counts.shape[0]
-    lane = lax.iota(jnp.int32, clusters)
-    placed = jnp.where(lane // share == lax.axis_index("row"), jnp.tile(counts, n), 0)
-    meta = jnp.concatenate([(cluster_ids << (n * docs - 1).bit_length()) + member_order, placed]).reshape(1, -1)
     vmem = functools.partial(pl.BlockSpec, memory_space=pltpu.VMEM)
     hbm = functools.partial(pl.BlockSpec, memory_space=pl.ANY)
     dma = pltpu.SemaphoreType.DMA
@@ -341,11 +357,15 @@
         functools.partial(kernel, n, lines),
         out_shape=(
             jax.ShapeDtypeStruct((1, docs), f32),
-            jax.ShapeDtypeStruct((clusters // n, 1), f32),
+            jax.ShapeDtypeStruct((1, clusters // n), f32),
         ),
-        in_specs=[hbm(), hbm(), vmem(), vmem()],
+        in_specs=[hbm()] * 6,
         out_specs=(vmem(), vmem()),
         scratch_shapes=[
+            pltpu.VMEM((docs,), i32),
+            pltpu.VMEM((docs,), i32),
+            pltpu.VMEM((clusters,), i32),
+            pltpu.SMEM((share,), i32),
             pltpu.VMEM((docs, width), bf16),
             pltpu.VMEM((width, kept), bf16),
             pltpu.VMEM((n, docs, kept), bf16),
@@ -359,6 +379,7 @@
             pltpu.VMEM((lines, 1, docs), f32),
             pltpu.VMEM((planes, 1, docs), f32),
             pltpu.VMEM((n, 1, clusters), f32),
+            dma((4,)),
             dma((CHUNKS,)),
             dma,
             dma((4, CHUNKS)),
@@ -376,10 +397,10 @@
             dma((n,)),
         ],
         compiler_params=pltpu.CompilerParams(
-            collective_id=0, has_side_effects=True, vmem_limit_bytes=48 * 1024 * 1024
+            collective_id=0, has_side_effects=True, vmem_limit_bytes=63 * 1024 * 1024
         ),
         name="cluster_scores",
-    )(embeddings, basis, meta, owner_map.reshape(1, -1))
+    )(embeddings, basis, cluster_ids, member_order, owner_map, counts)
     return best.reshape(-1), scores.reshape(-1)
 
 

time: 39.6 us -> 38.3 us (0.967)
  other arithmetic: 1.34 us -> 0 us
  Pallas kernels: 33.9 us -> 35.1 us
  local copies, waits for them, and re-layouts: 3.57 us -> 2.39 us
    pallas_call x1, Pallas kernels: 33.9 us -> 35.1 us  [body(): pl.pallas_call(functools.partial(kernel, n, lines), out_shape=(jax.ShapeD...]
    another operation x2 -> x0, local copies, waits for them, and re-layouts: 0.74 us -> none  [body(): jnp.tile(counts, n)]
    add x1 -> x0, other arithmetic: 0.7 us -> none  [body(): (cluster_ids << (n * docs - 1).bit_length()) + member_order]
    pallas_call x1 -> x0, other arithmetic: 0.63 us -> none  [body(): pl.pallas_call(functools.partial(kernel, n, lines), out_shape=(jax.ShapeD...]
    unnamed x5 -> x2, local copies, waits for them, and re-layouts: 2.82 us -> 2.39 us
where the time goes in v2:
time: 38.3 us; the launch traced here: 38.1 us
  Pallas kernels  35.1 us (92%)
  local copies, waits for them, and re-layouts  2.39 us (6%)
  between operations  0.64 us (2%)
    pallas_call x1, Pallas kernels, body(): pl.pallas_call(functools.partial(kernel, n, lines), out_shape=(jax.ShapeD...  35.1 us
    unnamed x2, local copies, waits for them, and re-layouts  2.39 us

profile of v2, /device:TPU:0, one launch (start us, length us, event | category | flops | bytes accessed | tf_op | source)
XLA Modules:
  0.0 38.1 jit_solution(4585183878776964646)
XLA Ops:
  0.6 35.1 %cluster_scores.1 = (f32[1,512]{1,0:T(1,128)}, f32[1,8]{1,0:T(1,128)}) custom-call(bf16[512,4096]{1,0:T(8,128)(2,1)} %emb_hbm.1, bf16[4096,256]{1,0:T(8,128)(2,1)} %basis_hbm.1, s32[512]{0:T(512)} %ids_hbm.1, s32[512]{0:T(512)} %order_hbm.1, s32[128]{0:T(128)} %owner_hbm.1, s32[8]{0:T(128)} %counts_hbm.1), custom_call_target="tpu_custom_call" | custom-call | tf_op jit(solution)/shard_map/cluster_scores/pallas_call | solution.py:356
  35.7 1.2 %copy.10 = f32[512]{0:T(512)} copy(f32[512]{0:T(512)} %bitcast.2) | data formatting | bytes 4096
  37.0 1.1 %copy.11 = f32[8]{0:T(128)} copy(f32[8]{0:T(128)} %bitcast.3) | data formatting | bytes 64

commit v3 on v2

--- a/solution.py
+++ b/solution.py
@@ -23,7 +23,7 @@
 def kernel(
     n, lines, emb_hbm, basis_hbm, ids_hbm, order_hbm, owner_hbm, counts_hbm,
     best_ref, scores_ref,
-    ids, order, owner, counts_here, emb, basis, blk, meta, kcol, ccol, acc, col, row, home, rr, rc, part,
+    ids, order, owner, counts_here, emb, basis, blk, meta, kcol, ccol, acc, col, row, home, rr, rc, plane_part, line_part,
     small_sem, load_sem, basis_sem, own_send, plane_recv, fwd_plane, line_recv, fwd_send,
     meta_send, meta_recv, row_send, row_recv, col_send, col_recv, part_send, part_recv,
 ):
@@ -74,31 +74,14 @@
         load.start()
         loads.append(load)
 
+    mates = [(q, me ^ q) for q in range(1, lines)]
+    mates += [(lines + k, lax.rem(z + k, planes) * lines + line) for k in range(1, planes)]
     barrier = pltpu.get_barrier_semaphore()
-
-    @pl.loop(1, n)
-    def _(k):
-        pl.semaphore_signal(barrier, inc=1, device_id={"row": (me + k) % n}, device_id_type=MESH)
-
-    pl.semaphore_wait(barrier, n - 1)
-
-    for copy in smalls:
-        copy.wait()
-    own_ids = ids[...].reshape(1, docs)
-    own_order = order[...].reshape(1, docs)
-    meta[me, :, :docs] = lax.shift_left(own_ids, order_bits) + own_order
-    lane = lax.broadcasted_iota(jnp.int32, (1, clusters), 1) - me * share
-    placed = jnp.zeros((1, clusters), jnp.int32)
-    for k in range(share):
-        placed = jnp.where(lane == k, counts_here[k], placed)
-    meta[me, :, docs:] = placed
-
-    def meta_copy(k):
-        return remote(meta.at[me], meta.at[me], meta_send.at[k], meta_recv.at[me], (me + k) % n)
-
-    @pl.loop(1, n)
-    def _(k):
-        meta_copy(k).start()
+    for _, d in mates:
+        pl.semaphore_signal(barrier, inc=1, device_id={"row": d}, device_id_type=MESH)
+
+    def meta_copy(i, d):
+        return remote(meta.at[me], meta.at[me], meta_send.at[i], meta_recv.at[me], d)
 
     goes_up = from_below(z, z + 1)
     goes_down = from_above(z, z - 1)
@@ -129,20 +112,44 @@
         )
         scale = lax.rsqrt(jnp.sum(projected * projected, axis=1, keepdims=True) + epsilon)
         blk[me, pl.ds(c * size, size), :] = (projected * scale).astype(jnp.bfloat16)
+        if c == 0:
+            pl.semaphore_wait(barrier, len(mates))
         each(own_copies(c)[::-1], lambda copy: copy.start())
 
-    @pl.loop(1, n)
-    def _(k):
-        d = (me + k) % n
-        remote(meta.at[d], meta.at[d], meta_send.at[k], meta_recv.at[d], d).wait_recv()
+    for copy in smalls:
+        copy.wait()
+    own_ids = ids[...].reshape(1, docs)
+    own_order = order[...].reshape(1, docs)
+    meta[me] = lax.shift_left(own_ids, order_bits) + own_order
+    for i, d in mates:
+        meta_copy(i, d).start()
+    acc[...] = jnp.full_like(acc, -1.0)
+    lane = lax.broadcasted_iota(jnp.int32, (1, clusters), 1) - me * share
+    placed = jnp.zeros((1, clusters), jnp.int32)
+    for k in range(share):
+        placed = jnp.where(lane == k, counts_here[k], placed)
+    plane_part[line, :, clusters:] = placed.astype(jnp.float32)
+
+    owned = (owner[...].reshape(1, clusters) == me).astype(jnp.float32)
+    before = (
+        lax.broadcasted_iota(jnp.int32, (clusters, clusters), 0)
+        < lax.broadcasted_iota(jnp.int32, (clusters, clusters), 1)
+    ).astype(jnp.bfloat16)
+    per_owner = clusters // n
+    many = jnp.broadcast_to(owned, (per_owner, clusters))
+    rank = jnp.dot(many.astype(jnp.bfloat16), before, preferred_element_type=jnp.float32)
+    wanted = lax.broadcasted_iota(jnp.int32, (per_owner, clusters), 0).astype(jnp.float32)
+    pick = (many > 0.5) & (rank == wanted)
+
+    for i, d in mates:
+        remote(meta.at[d], meta.at[d], meta_send.at[i], meta_recv.at[d], d).wait_recv()
 
     for p in range(lines):
-        keys = meta[z * lines + p][:, :docs]
+        keys = meta[z * lines + p]
         for i in range(0, docs, 128):
             column = jnp.transpose(jnp.broadcast_to(keys[:, i : i + 128], (128, 128)))
             kcol[pl.ds(p * docs + i, 128), :] = column
             ccol[pl.ds(p * docs + i, 128), :] = group_of(column)
-    acc[...] = jnp.full_like(acc, -1.0)
 
     def plane_wait(p, c):
         block_copy(z * lines + p, c, own_send.at[0, c], plane_recv.at[p, c], me ^ 1).wait_recv()
@@ -250,14 +257,14 @@
                 forward_step(k + 1, c)
             process_step(k)
 
-    for p in range(lines):
-        row[p] = row_of(acc[p * docs : (p + 1) * docs, :], jnp.max)
-
     def row_copy(q):
         return remote(row.at[line ^ q], rr.at[line], row_send.at[q], row_recv.at[line], me ^ q)
 
-    for q in range(1, lines):
-        row_copy(q).start()
+    for q in [*range(lines - 1, 0, -1), 0]:
+        rows = pl.ds(pl.multiple_of((line ^ q) * docs, docs), docs)
+        row[line ^ q] = row_of(acc[rows, :], jnp.max)
+        if q:
+            row_copy(q).start()
     home[...] = jnp.maximum(home[...], row[line])
     for q in range(1, lines):
         remote(row.at[line], rr.at[line ^ q], row_send.at[q], row_recv.at[line ^ q], me ^ q).wait_recv()
@@ -279,37 +286,31 @@
         total = jnp.zeros((128, 128), jnp.float32)
         for j in range(0, docs, 128):
             total += jnp.where(ids_row == own_ids[:, j : j + 128], adds[:, j : j + 128], 0.0)
-        part[me, :, i : i + 128] = row_of(total, jnp.sum)
-
-    def part_copy(k):
-        return remote(part.at[me], part.at[me], part_send.at[k], part_recv.at[me], (me + k) % n)
-
-    @pl.loop(1, n)
-    def _(k):
-        part_copy(k).start()
-
-    owned = (owner[...].reshape(1, clusters) == me).astype(jnp.float32)
-    before = (
-        lax.broadcasted_iota(jnp.int32, (clusters, clusters), 0)
-        < lax.broadcasted_iota(jnp.int32, (clusters, clusters), 1)
-    ).astype(jnp.bfloat16)
-    per_owner = clusters // n
-    many = jnp.broadcast_to(owned, (per_owner, clusters))
-    rank = jnp.dot(many.astype(jnp.bfloat16), before, preferred_element_type=jnp.float32)
-    wanted = lax.broadcasted_iota(jnp.int32, (per_owner, clusters), 0).astype(jnp.float32)
-    pick = (many > 0.5) & (rank == wanted)
-
-    @pl.loop(1, n)
-    def _(k):
-        d = (me + k) % n
-        remote(part.at[d], part.at[d], part_send.at[k], part_recv.at[d], d).wait_recv()
-
-    sums = jnp.zeros((1, clusters), jnp.float32)
-    counts = jnp.zeros((1, clusters), jnp.int32)
-    for d in range(n):
-        sums += part[d]
-        counts += meta[d][:, docs:]
-    mean = sums / counts.astype(jnp.float32)
+        plane_part[line, :, i : i + 128] = row_of(total, jnp.sum)
+
+    def plane_part_copy(q):
+        return remote(
+            plane_part.at[line], plane_part.at[line], part_send.at[q], part_recv.at[line], me ^ q
+        )
+
+    def line_part_copy(i, d):
+        return remote(
+            line_part.at[z], line_part.at[z], part_send.at[i], part_recv.at[lines + z], d
+        )
+
+    for q in range(lines - 1, 0, -1):
+        plane_part_copy(q).start()
+    for q in range(1, lines):
+        there = plane_part.at[line ^ q]
+        remote(there, there, part_send.at[q], part_recv.at[line ^ q], me ^ q).wait_recv()
+    line_part[z] = sum(plane_part[p] for p in range(lines))
+    for i, d in mates[lines - 1 :]:
+        line_part_copy(i, d).start()
+    for i, d in mates[lines - 1 :]:
+        there = line_part.at[d // lines]
+        remote(there, there, part_send.at[i], part_recv.at[lines + d // lines], d).wait_recv()
+    totals = sum(line_part[at] for at in range(planes))
+    mean = totals[:, :clusters] / totals[:, clusters:]
     picked = jnp.where(pick, mean, 0.0)
     folded = sum(picked[:, i : i + 128] for i in range(0, clusters, 128))
     rest = jnp.zeros((128 - per_owner, 128), jnp.float32)
@@ -320,10 +321,12 @@
         if lines == 4:
             diagonal_copy(c).wait_send()
 
-    @pl.loop(1, n)
-    def _(k):
-        meta_copy(k).wait_send()
-        part_copy(k).wait_send()
+    for i, d in mates:
+        meta_copy(i, d).wait_send()
+    for q in range(1, lines):
+        plane_part_copy(q).wait_send()
+    for i, d in mates[lines - 1 :]:
+        line_part_copy(i, d).wait_send()
 
     for q in range(1, lines):
         row_copy(q).wait_send()
@@ -369,7 +372,7 @@
             pltpu.VMEM((docs, width), bf16),
             pltpu.VMEM((width, kept), bf16),
             pltpu.VMEM((n, docs, kept), bf16),
-            pltpu.VMEM((n, 1, docs + clusters), i32),
+            pltpu.VMEM((n, 1, docs), i32),
             pltpu.VMEM((lines * docs, 128), i32),
             pltpu.VMEM((lines * docs, 128), i32),
             pltpu.VMEM((lines * docs, 128), f32),
@@ -378,7 +381,8 @@
             pltpu.VMEM((1, docs), f32),
             pltpu.VMEM((lines, 1, docs), f32),
             pltpu.VMEM((planes, 1, docs), f32),
-            pltpu.VMEM((n, 1, clusters), f32),
+            pltpu.VMEM((lines, 1, 2 * clusters), f32),
+            pltpu.VMEM((planes, 1, 2 * clusters), f32),
             dma((4,)),
             dma((CHUNKS,)),
             dma,
@@ -387,17 +391,17 @@
             dma((CHUNKS,)),
             dma((planes, CHUNKS)),
             dma((planes, CHUNKS)),
-            dma((n,)),
+            dma((lines + planes,)),
             dma((n,)),
             dma((lines,)),
             dma((lines,)),
             dma((planes,)),
             dma((planes,)),
-            dma((n,)),
-            dma((n,)),
+            dma((lines + planes,)),
+            dma((lines + planes,)),
         ],
         compiler_params=pltpu.CompilerParams(
-            collective_id=0, has_side_effects=True, vmem_limit_bytes=63 * 1024 * 1024
+            collective_id=0, has_side_effects=True, vmem_limit_bytes=62 * 1024 * 1024 + 512 * 1024
         ),
         name="cluster_scores",
     )(embeddings, basis, cluster_ids, member_order, owner_map, counts)

time: 38.3 us -> 42.7 us (1.11)
  Pallas kernels: 35.1 us -> 39.5 us
    pallas_call x1, Pallas kernels: 35.1 us -> 39.5 us  [body(): pl.pallas_call(functools.partial(kernel, n, lines), out_shape=(jax.ShapeD...]
where the time goes in v3:
time: 42.7 us; the launch traced here: 42.6 us
  Pallas kernels  39.5 us (93%)
  local copies, waits for them, and re-layouts  2.39 us (6%)
  between operations  0.64 us (1%)
    pallas_call x1, Pallas kernels, body(): pl.pallas_call(functools.partial(kernel, n, lines), out_shape=(jax.ShapeD...  39.5 us
    unnamed x2, local copies, waits for them, and re-layouts  2.39 us

profile of v3, /device:TPU:0, one launch (start us, length us, event | category | flops | bytes accessed | tf_op | source)
XLA Modules:
  0.0 42.6 jit_solution(17725143642933564171)
XLA Ops:
  0.6 39.5 %cluster_scores.1 = (f32[1,512]{1,0:T(1,128)}, f32[1,8]{1,0:T(1,128)}) custom-call(bf16[512,4096]{1,0:T(8,128)(2,1)} %emb_hbm.1, bf16[4096,256]{1,0:T(8,128)(2,1)} %basis_hbm.1, s32[512]{0:T(512)} %ids_hbm.1, s32[512]{0:T(512)} %order_hbm.1, s32[128]{0:T(128)} %owner_hbm.1, s32[8]{0:T(128)} %counts_hbm.1), custom_call_target="tpu_custom_call" | custom-call | tf_op jit(solution)/shard_map/cluster_scores/pallas_call | solution.py:359
  40.2 1.2 %copy.10 = f32[512]{0:T(512)} copy(f32[512]{0:T(512)} %bitcast.2) | data formatting | bytes 4096
  41.4 1.1 %copy.11 = f32[8]{0:T(128)} copy(f32[8]{0:T(128)} %bitcast.3) | data formatting | bytes 64

commit v4 on v3

--- a/solution.py
+++ b/solution.py
@@ -23,12 +23,13 @@
 def kernel(
     n, lines, emb_hbm, basis_hbm, ids_hbm, order_hbm, owner_hbm, counts_hbm,
     best_ref, scores_ref,
-    ids, order, owner, counts_here, emb, basis, blk, meta, kcol, ccol, acc, col, row, home, rr, rc, plane_part, line_part,
+    ids, order, owner, counts_here, emb, basis, blk, meta, kcol, ccol, acc, col, row, home, rr, rc, part,
     small_sem, load_sem, basis_sem, own_send, plane_recv, fwd_plane, line_recv, fwd_send,
     meta_send, meta_recv, row_send, row_recv, col_send, col_recv, part_send, part_recv,
 ):
     planes = n // lines
     half = planes // 2
+    direct = False
     docs = blk.shape[1]
     size = docs // CHUNKS
     clusters = owner_hbm.shape[0]
@@ -77,11 +78,18 @@
     mates = [(q, me ^ q) for q in range(1, lines)]
     mates += [(lines + k, lax.rem(z + k, planes) * lines + line) for k in range(1, planes)]
     barrier = pltpu.get_barrier_semaphore()
-    for _, d in mates:
+    everyone = [(k, lax.rem(me + k, n)) for k in range(n - 1, 0, -1)]
+    for _, d in everyone:
         pl.semaphore_signal(barrier, inc=1, device_id={"row": d}, device_id_type=MESH)
 
     def meta_copy(i, d):
         return remote(meta.at[me], meta.at[me], meta_send.at[i], meta_recv.at[me], d)
+
+    for copy in smalls:
+        copy.wait()
+    own_ids = ids[...].reshape(1, docs)
+    own_order = order[...].reshape(1, docs)
+    meta[me] = lax.shift_left(own_ids, order_bits) + own_order
 
     goes_up = from_below(z, z + 1)
     goes_down = from_above(z, z - 1)
@@ -95,6 +103,12 @@
             down = jnp.maximum(me - lines, 0)
             copies.append((goes_up, block_copy(me, c, own_send.at[2, c], line_recv.at[z, c], up)))
             copies.append((goes_down, block_copy(me, c, own_send.at[3, c], line_recv.at[z, c], down)))
+        if direct:
+            copies = copies[::-1]
+            up = jnp.minimum(me + 2 * lines, n - 1)
+            down = jnp.maximum(me - 2 * lines, 0)
+            copies.append((from_below(z, z + 2), block_copy(me, c, own_send.at[4, c], line_recv.at[z, c], up)))
+            copies.append((z == planes - 1, block_copy(me, c, own_send.at[5, c], line_recv.at[z, c], down)))
         return copies
 
     def each(copies, act):
@@ -103,6 +117,10 @@
                 act(copy)
             else:
                 pl.when(condition)(functools.partial(act, copy))
+
+    pl.semaphore_wait(barrier, n - 1)
+    for i, d in mates:
+        meta_copy(i, d).start()
 
     basis_copy.wait()
     for c in range(CHUNKS):
@@ -112,23 +130,14 @@
         )
         scale = lax.rsqrt(jnp.sum(projected * projected, axis=1, keepdims=True) + epsilon)
         blk[me, pl.ds(c * size, size), :] = (projected * scale).astype(jnp.bfloat16)
-        if c == 0:
-            pl.semaphore_wait(barrier, len(mates))
         each(own_copies(c)[::-1], lambda copy: copy.start())
 
-    for copy in smalls:
-        copy.wait()
-    own_ids = ids[...].reshape(1, docs)
-    own_order = order[...].reshape(1, docs)
-    meta[me] = lax.shift_left(own_ids, order_bits) + own_order
-    for i, d in mates:
-        meta_copy(i, d).start()
     acc[...] = jnp.full_like(acc, -1.0)
     lane = lax.broadcasted_iota(jnp.int32, (1, clusters), 1) - me * share
     placed = jnp.zeros((1, clusters), jnp.int32)
     for k in range(share):
         placed = jnp.where(lane == k, counts_here[k], placed)
-    plane_part[line, :, clusters:] = placed.astype(jnp.float32)
+    part[me, :, clusters:] = placed.astype(jnp.float32)
 
     owned = (owner[...].reshape(1, clusters) == me).astype(jnp.float32)
     before = (
@@ -164,6 +173,16 @@
         low, high = z - k, z + k
         below = from_below(low, z)
         above = from_above(high, z)
+        if direct:
+            return (
+                (jnp.maximum(low, 0), below, below & (z < 0), jnp.minimum(me + lines, n - 1)),
+                (
+                    jnp.minimum(high, planes - 1),
+                    above,
+                    above & (z == planes - 2),
+                    jnp.maximum(me - 2 * lines, 0),
+                ),
+            )
         return (
             (jnp.maximum(low, 0), below, below & from_below(low, z + 1), jnp.minimum(me + lines, n - 1)),
             (jnp.minimum(high, planes - 1), above, above & from_above(high, z - 1), jnp.maximum(me - lines, 0)),
@@ -217,7 +236,7 @@
                 acc[rows, :] = row_part
             return jnp.maximum(carry, jnp.concatenate(outs, axis=1))
 
-        result = lax.fori_loop(0, lines, one, jnp.full((1, size), -1.0, jnp.float32))
+        result = lax.fori_loop(0, lines, one, jnp.full((1, size), -1.0, jnp.float32), unroll=True)
         if visitor:
             col[s, :, at] = result
         else:
@@ -286,30 +305,16 @@
         total = jnp.zeros((128, 128), jnp.float32)
         for j in range(0, docs, 128):
             total += jnp.where(ids_row == own_ids[:, j : j + 128], adds[:, j : j + 128], 0.0)
-        plane_part[line, :, i : i + 128] = row_of(total, jnp.sum)
-
-    def plane_part_copy(q):
-        return remote(
-            plane_part.at[line], plane_part.at[line], part_send.at[q], part_recv.at[line], me ^ q
-        )
-
-    def line_part_copy(i, d):
-        return remote(
-            line_part.at[z], line_part.at[z], part_send.at[i], part_recv.at[lines + z], d
-        )
-
-    for q in range(lines - 1, 0, -1):
-        plane_part_copy(q).start()
-    for q in range(1, lines):
-        there = plane_part.at[line ^ q]
-        remote(there, there, part_send.at[q], part_recv.at[line ^ q], me ^ q).wait_recv()
-    line_part[z] = sum(plane_part[p] for p in range(lines))
-    for i, d in mates[lines - 1 :]:
-        line_part_copy(i, d).start()
-    for i, d in mates[lines - 1 :]:
-        there = line_part.at[d // lines]
-        remote(there, there, part_send.at[i], part_recv.at[lines + d // lines], d).wait_recv()
-    totals = sum(line_part[at] for at in range(planes))
+        part[me, :, i : i + 128] = row_of(total, jnp.sum)
+
+    def part_copy(k, d):
+        return remote(part.at[me], part.at[me], part_send.at[k], part_recv.at[me], d)
+
+    for k, d in everyone:
+        part_copy(k, d).start()
+    for k, d in everyone:
+        remote(part.at[d], part.at[d], part_send.at[k], part_recv.at[d], d).wait_recv()
+    totals = sum(part[d] for d in range(n))
     mean = totals[:, :clusters] / totals[:, clusters:]
     picked = jnp.where(pick, mean, 0.0)
     folded = sum(picked[:, i : i + 128] for i in range(0, clusters, 128))
@@ -323,10 +328,8 @@
 
     for i, d in mates:
         meta_copy(i, d).wait_send()
-    for q in range(1, lines):
-        plane_part_copy(q).wait_send()
-    for i, d in mates[lines - 1 :]:
-        line_part_copy(i, d).wait_send()
+    for k, d in everyone:
+        part_copy(k, d).wait_send()
 
     for q in range(1, lines):
         row_copy(q).wait_send()
@@ -381,12 +384,11 @@
             pltpu.VMEM((1, docs), f32),
             pltpu.VMEM((lines, 1, docs), f32),
             pltpu.VMEM((planes, 1, docs), f32),
-            pltpu.VMEM((lines, 1, 2 * clusters), f32),
-            pltpu.VMEM((planes, 1, 2 * clusters), f32),
+            pltpu.VMEM((n, 1, 2 * clusters), f32),
             dma((4,)),
             dma((CHUNKS,)),
             dma,
-            dma((4, CHUNKS)),
+            dma((6, CHUNKS)),
             dma((lines, CHUNKS)),
             dma((CHUNKS,)),
             dma((planes, CHUNKS)),
@@ -397,8 +399,8 @@
             dma((lines,)),
             dma((planes,)),
             dma((planes,)),
-            dma((lines + planes,)),
-            dma((lines + planes,)),
+            dma((n,)),
+            dma((n,)),
         ],
         compiler_params=pltpu.CompilerParams(
             collective_id=0, has_side_effects=True, vmem_limit_bytes=62 * 1024 * 1024 + 512 * 1024

time: 42.7 us -> 37.8 us (0.89)
  Pallas kernels: 39.5 us -> 34.5 us
    pallas_call x1, Pallas kernels: 39.5 us -> 34.5 us  [body(): pl.pallas_call(functools.partial(kernel, n, lines), out_shape=(jax.ShapeD...]
where the time goes in v4:
time: 37.8 us; the launch traced here: 37.6 us
  Pallas kernels  34.5 us (91%)
  local copies, waits for them, and re-layouts  2.39 us (6%)
  between operations  0.64 us (2%)
    pallas_call x1, Pallas kernels, body(): pl.pallas_call(functools.partial(kernel, n, lines), out_shape=(jax.ShapeD...  34.5 us
    unnamed x2, local copies, waits for them, and re-layouts  2.39 us

profile of v4, /device:TPU:0, one launch (start us, length us, event | category | flops | bytes accessed | tf_op | source)
XLA Modules:
  0.0 37.6 jit_solution(12813485370126376246)
XLA Ops:
  0.6 34.5 %cluster_scores.1 = (f32[1,512]{1,0:T(1,128)}, f32[1,8]{1,0:T(1,128)}) custom-call(bf16[512,4096]{1,0:T(8,128)(2,1)} %emb_hbm.1, bf16[4096,256]{1,0:T(8,128)(2,1)} %basis_hbm.1, s32[512]{0:T(512)} %ids_hbm.1, s32[512]{0:T(512)} %order_hbm.1, s32[128]{0:T(128)} %owner_hbm.1, s32[8]{0:T(128)} %counts_hbm.1), custom_call_target="tpu_custom_call" | custom-call | tf_op jit(solution)/shard_map/cluster_scores/pallas_call | solution.py:362
  35.2 1.2 %copy.10 = f32[512]{0:T(512)} copy(f32[512]{0:T(512)} %bitcast.2) | data formatting | bytes 4096
  36.4 1.1 %copy.11 = f32[8]{0:T(128)} copy(f32[8]{0:T(128)} %bitcast.3) | data formatting | bytes 64

commit v5 on v4

--- a/solution.py
+++ b/solution.py
@@ -118,20 +118,6 @@
             else:
                 pl.when(condition)(functools.partial(act, copy))
 
-    pl.semaphore_wait(barrier, n - 1)
-    for i, d in mates:
-        meta_copy(i, d).start()
-
-    basis_copy.wait()
-    for c in range(CHUNKS):
-        loads[c].wait()
-        projected = jnp.dot(
-            emb[pl.ds(c * size, size), :], basis[...], preferred_element_type=jnp.float32
-        )
-        scale = lax.rsqrt(jnp.sum(projected * projected, axis=1, keepdims=True) + epsilon)
-        blk[me, pl.ds(c * size, size), :] = (projected * scale).astype(jnp.bfloat16)
-        each(own_copies(c)[::-1], lambda copy: copy.start())
-
     acc[...] = jnp.full_like(acc, -1.0)
     lane = lax.broadcasted_iota(jnp.int32, (1, clusters), 1) - me * share
     placed = jnp.zeros((1, clusters), jnp.int32)
@@ -149,6 +135,21 @@
     rank = jnp.dot(many.astype(jnp.bfloat16), before, preferred_element_type=jnp.float32)
     wanted = lax.broadcasted_iota(jnp.int32, (per_owner, clusters), 0).astype(jnp.float32)
     pick = (many > 0.5) & (rank == wanted)
+
+    pl.semaphore_wait(barrier, n - 1)
+    for i, d in mates:
+        meta_copy(i, d).start()
+
+    basis_copy.wait()
+    for c in range(CHUNKS):
+        loads[c].wait()
+        projected = jnp.dot(
+            emb[pl.ds(c * size, size), :], basis[...], preferred_element_type=jnp.float32
+        )
+        scale = lax.rsqrt(jnp.sum(projected * projected, axis=1, keepdims=True) + epsilon)
+        blk[me, pl.ds(c * size, size), :] = (projected * scale).astype(jnp.bfloat16)
+        each(own_copies(c)[::-1], lambda copy: copy.start())
+
 
     for i, d in mates:
         remote(meta.at[d], meta.at[d], meta_send.at[i], meta_recv.at[d], d).wait_recv()

time: 37.8 us -> 37.8 us (level)
  no operation moved by 1% of the time
where the time goes in v5:
time: 37.8 us; the launch traced here: 37.6 us
  Pallas kernels  34.5 us (91%)
  local copies, waits for them, and re-layouts  2.39 us (6%)
  between operations  0.64 us (2%)
    pallas_call x1, Pallas kernels, body(): pl.pallas_call(functools.partial(kernel, n, lines), out_shape=(jax.ShapeD...  34.5 us
    unnamed x2, local copies, waits for them, and re-layouts  2.39 us

profile of v5, /device:TPU:0, one launch (start us, length us, event | category | flops | bytes accessed | tf_op | source)
XLA Modules:
  0.0 37.6 jit_solution(12936639972166223606)
XLA Ops:
  0.6 34.5 %cluster_scores.1 = (f32[1,512]{1,0:T(1,128)}, f32[1,8]{1,0:T(1,128)}) custom-call(bf16[512,4096]{1,0:T(8,128)(2,1)} %emb_hbm.1, bf16[4096,256]{1,0:T(8,128)(2,1)} %basis_hbm.1, s32[512]{0:T(512)} %ids_hbm.1, s32[512]{0:T(512)} %order_hbm.1, s32[128]{0:T(128)} %owner_hbm.1, s32[8]{0:T(128)} %counts_hbm.1), custom_call_target="tpu_custom_call" | custom-call | tf_op jit(solution)/shard_map/cluster_scores/pallas_call | solution.py:363
  35.2 1.2 %copy.10 = f32[512]{0:T(512)} copy(f32[512]{0:T(512)} %bitcast.2) | data formatting | bytes 4096
  36.4 1.1 %copy.11 = f32[8]{0:T(128)} copy(f32[8]{0:T(128)} %bitcast.3) | data formatting | bytes 64
